TPU v7x, 32 devices: a whole 2x2x4 slice. The times are simulated.
32 devices in a mesh: groups: 2 (over y), spec: 4 (over z), band: 2 (over x), sub: 2 (over core).
Axes of the slice: x: 2, y: 2, z: 4, core: 2. Of those that a mesh axis runs over, the one named last changes fastest.
Arguments:
- spectrum: float32 [3456, 32, 512], P(('groups', 'spec'), 'band', 'sub'), parts along dimension 0, may hold values from 0.05 to 2
- wind_speed: float32 [4, 2, 4, 1024], P(('groups', 'band'), 'sub', 'spec'), parts along dimension 0, may hold values from 3 to 25
- wind_dir: float32 [4, 2, 4, 1024], P(('groups', 'band'), 'sub', 'spec'), parts along dimension 0, may hold values from -3.140625 to 3.140625
- ice_mask: int32 [4, 2, 4, 1024], P(('groups', 'band'), 'sub', 'spec'), parts along dimension 0, may hold values 0 or 1
- depth_class: int32 [4, 2, 4, 1024], P(('groups', 'band'), 'sub', 'spec'), parts along dimension 0, may hold values from 0 to 15
- bottom_table: float32 [16, 48], replicated, may hold values from 0.01 to 0.2
- sea_slots: int32 [4, 2, 4, 768], P(('groups', 'band'), 'sub', 'spec'), parts along dimension 0, may hold values from 0 to 1023, as said below
- sea_count: int32 [4, 2, 4, 1], P(('groups', 'band'), 'sub', 'spec'), parts along dimension 0, may hold values from 341 to 768, as said below
Outputs:
- advanced: float32 [3456, 32, 512], P(('groups', 'spec'), 'band', 'sub'), parts along dimension 0
There are 2 independent parts, one for each index of `groups`. A program takes and returns all parts, laid end to end along the dimension named above; an argument that names none is the same for every part. Nothing has to cross between parts.
Inputs may be any that keep to these rules, and one draw needn't show every extreme that they name: `sea_slots`: the 768 entries of one block's row are distinct positions of that block. `sea_count`: some block holds exactly 768 sea points.
All inputs are finite; a program needn't handle non-finite values. No bound on the sum of `ice_mask` on one device may be relied on, other than what follows from the above.
Results may differ from a plain program's by a relative error of at most 0.0003.
Values sent between devices are 32-bit elements; how exact they have to be, the bound alone decides.
A program may use at most 128 MiB of HBM per device.

v0:
```python
import math

import jax
import jax.numpy as jnp
from jax import lax
from jax.sharding import PartitionSpec as P

ND = 36
NF = 48


low_frequency = 0.04
growth_ratio = 1.07
courant_limit = 0.44
gravity = 9.81
wind_coef = 0.02
dissip_coef = 0.03
steep_ref = 0.4
quad_coef = 0.02
ice_rate = 0.5


def with_halo(block, sides, width, periodic):
    for axis, dim in sides:
        count = lax.axis_size(axis)
        forward = [(i, i + 1) for i in range(count - 1)]
        if periodic:
            forward.append((count - 1, 0))
        backward = [(target, source) for source, target in forward]
        low = lax.ppermute(
            lax.slice_in_dim(block, block.shape[dim] - width, None, axis=dim), axis, forward
        )
        high = lax.ppermute(lax.slice_in_dim(block, 0, width, axis=dim), axis, backward)
        block = jnp.concatenate([low, block, high], axis=dim)
    return block


def frequencies(index):
    return low_frequency * jnp.exp(index * math.log(growth_ratio))


def shifted(values, dir_turn, offset):
    rolled = jnp.roll(values, dir_turn, axis=0)
    count_freqs = values.shape[1]
    if offset > 0:
        padding = jnp.zeros((values.shape[0], offset) + values.shape[2:], values.dtype)
        return jnp.concatenate([padding, rolled[:, : count_freqs - offset]], axis=1)
    padding = jnp.zeros((values.shape[0], -offset) + values.shape[2:], values.dtype)
    return jnp.concatenate([rolled[:, -offset:], padding], axis=1)


def source_step(spectrum, wind_speed, wind_dir, ice_flag, depth_class, sea_flag, bottom_table):
    count_dirs, count_freqs = (spectrum.shape[0], spectrum.shape[1])
    frequency = frequencies(jnp.arange(count_freqs, dtype=jnp.float32))
    bin_width = frequency * (growth_ratio - 1.0 / growth_ratio) * 0.5 * (2.0 * math.pi / count_dirs)
    angles = jnp.arange(count_dirs, dtype=jnp.float32) * (2.0 * math.pi / count_dirs)
    energy_sum = jnp.sum(spectrum * bin_width[None, :, None], axis=(0, 1))
    inverse_sum = jnp.sum(spectrum * (bin_width / frequency)[None, :, None], axis=(0, 1))
    mean_freq = energy_sum / inverse_sum
    mean_wave = mean_freq * mean_freq * (4.0 * math.pi**2 / gravity)
    steepness = energy_sum * mean_wave * mean_wave
    ice_float = ice_flag.astype(jnp.float32)
    open_water = 1.0 - ice_float
    inverse_speed = frequency * (2.0 * math.pi / gravity)
    alignment = jnp.cos(angles[:, None] - wind_dir[None, :])
    wind_ratio = wind_speed[None, None, :] * inverse_speed[None, :, None] * alignment[:, None, :]
    wind_growth = wind_coef * jnp.maximum(wind_ratio - 1.0, 0.0) * open_water[None, None, :]
    dissipation = (
        dissip_coef
        * (frequency[:, None] / mean_freq[None, :])
        * (steepness / steep_ref)[None, :] ** 2
        * open_water[None, :]
    )
    one_hot = (
        depth_class[None, :] == jnp.arange(bottom_table.shape[0], dtype=jnp.int32)[:, None]
    ).astype(jnp.float32)
    friction = jnp.dot(bottom_table.T, one_hot, precision=lax.Precision.HIGHEST)
    net_rate = wind_growth - dissipation[None] - friction[None]
    weights = (quad_coef * (frequency / frequency[-1]) ** 2)[None, :, None]
    center_sq = spectrum * spectrum
    plus_one = shifted(spectrum, -1, -3)
    minus_one = shifted(spectrum, 3, 4)
    plus_two = shifted(spectrum, 1, -3)
    minus_two = shifted(spectrum, -3, 4)
    quad_one = weights * (
        center_sq * (plus_one / 2.4414 + minus_one / 0.3164)
        - 2.0 * spectrum * plus_one * minus_one / 0.7725
    )
    quad_two = weights * (
        center_sq * (plus_two / 2.4414 + minus_two / 0.3164)
        - 2.0 * spectrum * plus_two * minus_two / 0.7725
    )
    transfer = (
        -2.0 * (quad_one + quad_two)
        + shifted(quad_one, 1, 3)
        + shifted(quad_one, -3, -4)
        + shifted(quad_two, -1, 3)
        + shifted(quad_two, 3, -4)
    )
    updated = jnp.maximum(spectrum * (1.0 + net_rate) + transfer, 0.0)
    damping = jnp.exp(-ice_rate * (frequency / frequency[-1]) ** 2)
    ice_factor = 1.0 - ice_float[None, :] * (1.0 - damping[:, None])
    return updated * ice_factor[None] * sea_flag[None, None, :]


def courant_numbers(dir_index, freq_index, latitude, count_dirs):
    ratio = low_frequency / frequencies(freq_index)
    angle = dir_index * (2.0 * math.pi / count_dirs)
    courant_x = courant_limit * (ratio * jnp.cos(angle))[:, None] / jnp.cos(latitude)[None, :]
    courant_y = courant_limit * ratio * jnp.sin(angle)
    return (courant_x, courant_y)


def latitudes(row_index, total_rows):
    degrees = -60.0 + 120.0 * (row_index + 0.5) / total_rows
    return degrees * (math.pi / 180.0)


def upwind_step(padded, courant_x, courant_y):
    center = padded[:, 1:-1, 1:-1]
    east = padded[:, 1:-1, 2:]
    west = padded[:, 1:-1, :-2]
    north = padded[:, 2:, 1:-1]
    south = padded[:, :-2, 1:-1]
    east_go = jnp.maximum(courant_x, 0.0)[:, :, None]
    west_go = jnp.minimum(courant_x, 0.0)[:, :, None]
    north_go = jnp.maximum(courant_y, 0.0)[:, None, None]
    south_go = jnp.minimum(courant_y, 0.0)[:, None, None]
    flux_east = east_go * center + west_go * east
    flux_west = east_go * west + west_go * center
    flux_north = north_go * center + south_go * north
    flux_south = north_go * south + south_go * center
    return center - (flux_east - flux_west) - (flux_north - flux_south)


def body(spectrum, wind_speed, wind_dir, ice_mask, depth_class, bottom_table, sea_slots, sea_count):
    local_comps, rows, cols = spectrum.shape
    spec_size = lax.axis_size("spec")
    block_len = rows * cols // spec_size
    most = sea_slots.shape[-1]
    all_slots, all_counts = (
        lax.all_gather(sea_slots, "spec", axis=2, tiled=True),
        lax.all_gather(sea_count, "spec", axis=2, tiled=True),
    )
    all_slots = all_slots.reshape(spec_size, most)
    all_counts = all_counts.reshape(spec_size, 1)
    slot_range = jnp.arange(most, dtype=jnp.int32)
    all_live = (slot_range[None, :] < all_counts).astype(jnp.float32)
    block_rows = jnp.arange(spec_size, dtype=jnp.int32)[:, None]
    sea_prop = (
        jnp.zeros((spec_size, block_len), jnp.float32).at[block_rows, all_slots].set(all_live)
    )
    my_slots = sea_slots.reshape(most)
    my_live = (slot_range < sea_count.reshape(())).astype(jnp.float32)
    speed_row = wind_speed.reshape(block_len)
    dir_row = wind_dir.reshape(block_len)
    ice_row = ice_mask.reshape(block_len)
    depth_row = depth_class.reshape(block_len)
    blocks = spectrum.reshape(local_comps, spec_size, block_len)
    gathered = lax.all_to_all(blocks, "spec", split_axis=1, concat_axis=0, tiled=True)
    sea_own = jnp.zeros((block_len,), jnp.float32).at[my_slots].set(my_live)
    sourced = source_step(
        gathered.reshape(ND, NF, block_len),
        speed_row,
        dir_row,
        ice_row,
        depth_row,
        sea_own,
        bottom_table,
    )
    stepped = lax.all_to_all(
        sourced.reshape(ND * NF, 1, block_len), "spec", split_axis=0, concat_axis=1, tiled=True
    )
    grid_part = stepped.reshape(local_comps, rows, cols)
    with_rows = with_halo(grid_part, (("band", 1),), 1, False)
    padded = with_halo(with_rows, (("sub", 2),), 1, True)
    comp_index = lax.axis_index("spec") * local_comps + jnp.arange(local_comps, dtype=jnp.int32)
    dir_index = (comp_index // NF).astype(jnp.float32)
    freq_index = (comp_index % NF).astype(jnp.float32)
    row_index = (lax.axis_index("band") * rows + jnp.arange(rows, dtype=jnp.int32)).astype(
        jnp.float32
    )
    latitude = latitudes(row_index, rows * lax.axis_size("band"))
    courant_x, courant_y = courant_numbers(dir_index, freq_index, latitude, ND)
    moved = upwind_step(padded, courant_x, courant_y)
    return moved * sea_prop.reshape(rows, cols)[None]


def solution(mesh):
    return jax.shard_map(
        body,
        mesh=mesh,
        in_specs=(
            P(("groups", "spec"), "band", "sub"),
            P(("groups", "band"), "sub", "spec", None),
            P(("groups", "band"), "sub", "spec", None),
            P(("groups", "band"), "sub", "spec", None),
            P(("groups", "band"), "sub", "spec", None),
            P(),
            P(("groups", "band"), "sub", "spec", None),
            P(("groups", "band"), "sub", "spec", None),
        ),
        out_specs=P(("groups", "spec"), "band", "sub"),
        check_vma=False,
    )
```

profile of v0, /device:TPU:0, one launch (start us, length us, event | category | flops | bytes accessed | tf_op | source)
XLA Modules:
  0.0 550.3 jit_solution(9441424204444950971)
XLA Ops:
  0.0 9.6 %reshape.429 = f32[432,4,1024]{2,1,0:T(4,128)} reshape(f32[432,16,256]{2,1,0:T(8,128)} %param.8) | data formatting | bytes 14155776 | tf_op jit(solution)/shard_map/reshape | solution.py:159
  9.7 10.0 %copy.19 = f32[432,4,1024]{2,0,1:T(8,128)} copy(f32[432,4,1024]{2,1,0:T(4,128)} %reshape.429) | data formatting | bytes 14155776 | tf_op jit(solution)/shard_map/reshape | solution.py:159
  19.7 6.5 %all-to-all-start = ((f32[432,4,1024]{2,0,1:T(8,128)}), f32[432,4,1024]{2,0,1:T(8,128)}, u32[]{:S(2)}, u32[]{:S(2)}) async-start(f32[432,4,1024]{2,0,1:T(8,128)} %copy.19), calls=%async_computation | async-start | bytes 14155776 | tf_op jit(solution)/shard_map/all_to_all | solution.py:160
  26.2 0.6 slice.112
  27.7 3.4 scatter_custom_fusion
  31.1 0.7 exponential_subtract_fusion
  31.8 0.6 subtract_cosine_fusion
  32.4 0.8 multiply_subtract_fusion
  33.2 0.8 broadcast_multiply_fusion
  33.9 1.0 convolution_bitcast_fusion
  34.9 147.0 %all-to-all-done = f32[432,4,1024]{2,0,1:T(8,128)} async-done(((f32[432,4,1024]{2,0,1:T(8,128)}), f32[432,4,1024]{2,0,1:T(8,128)}, u32[]{:S(2)}, u32[]{:S(2)}) %all-to-all-start) | async-done | bytes 7077920 | tf_op jit(solution)/shard_map/all_to_all | solution.py:160
  181.9 13.1 %fusion.48 = (f32[35,48,1024]{2,1,0:T(8,128)}, f32[35,48,1024]{2,1,0:T(8,128)}) fusion(f32[36,48,1024]{2,1,0:T(8,128)} %bitcast.2), kind=kLoop, calls=%fused_computation.113 | loop fusion | bytes 27525120 | tf_op jit(solution)/shard_map/jit(_roll_static)/slice | solution.py:43
  195.0 12.3 %fusion.51 = (f32[33,48,1024]{2,1,0:T(8,128)}, f32[33,48,1024]{2,1,0:T(8,128)}) fusion(f32[36,48,1024]{2,1,0:T(8,128)} %bitcast.2), kind=kLoop, calls=%fused_computation.116 | loop fusion | bytes 25952256 | tf_op jit(solution)/shard_map/jit(_roll_static)/slice | solution.py:43
  207.3 1.3 fusion.50
  208.6 1.0 fusion.49
  209.7 13.5 %subtract_multiply_fusion.1 = (f32[36,48,1024]{2,1,0:T(8,128)S(1)}, f32[36,48,1024]{2,1,0:T(8,128)S(1)}) fusion(f32[33,48,1024]{2,1,0:T(8,128)} %get-tuple-element.21, f32[3,48,1024]{2,1,0:T(8,128)S(1)} %get-tuple-element.19, f32[1,48,1024]{2,1,0:T(8,128)S(1)} %get-tuple-element.17, f32[35,48,1024]{2,1,0:T(8,128)} %get-tuple-element.15, ...), kind=kLoop, calls=%fused_computation.49 | loop fusion | flops 60162048 | bytes 49545408 | tf_op jit(solution)/shard_map/mul | solution.py:85
  223.2 3.5 slice.154
  226.7 3.3 slice.155
  230.0 3.5 slice.157
  233.6 3.2 slice.160
  236.9 0.7 slice.153
  237.6 0.7 slice.158
  238.3 4.1 fusion.21
  242.4 0.8 fusion.23
  243.2 13.5 %fusion.17 = f32[36,48,1024]{2,1,0:T(8,128)S(1)} fusion(f32[33,48,1024]{2,1,0:T(8,128)} %slice.160, f32[3,48,1024]{2,1,0:T(8,128)S(1)} %slice.159, f32[1,48,1024]{2,1,0:T(8,128)} %slice.158, f32[35,48,1024]{2,1,0:T(8,128)} %slice.157, f32[3,48,1024]{2,1,0:T(8,128)S(1)} %slice.156, f32[33,48,1024]{2,1,0:T(8,128)} %slice.155, f32[35,48,1024]{2,1,0:T(8,128)} %slice.154, ...), kind=kLoop, calls=%fused_computation.29 | loop fusion | flops 56623104 | bytes 57565184 | tf_op jit(solution)/shard_map/mul | solution.py:103
  256.7 13.8 %copy.20 = f32[1728,1,1024]{2,1,0:T(1,128)} copy(f32[1728,1,1024]{2,0,1:T(8,128)S(1)} %bitcast.35) | data formatting | bytes 14155776 | tf_op jit(solution)/shard_map/reshape | solution.py:172
  270.5 5.5 %all-to-all-start.1 = ((f32[1728,1,1024]{2,1,0:T(1,128)}), f32[1728,1,1024]{2,1,0:T(1,128)}, u32[]{:S(2)}, u32[]{:S(2)}) async-start(f32[1728,1,1024]{2,1,0:T(1,128)} %copy.20), calls=%async_computation.1 | async-start | bytes 14155776 | tf_op jit(solution)/shard_map/all_to_all | solution.py:171
  276.1 0.6 dynamic-slice
  276.7 0.6 bitcast_dynamic-update-slice_fusion
  277.4 153.6 %all-reduce.8 = s32[4]{0:T(128)S(1)} all-reduce(s32[4]{0:T(128)S(1)} %bitcast_dynamic-update-slice_fusion), channel_id=1, replica_groups=mesh['groups'=2,'spec'=4,'band'=2,'sub'=2] {'spec'}, use_global_device_ids=true, to_apply=%add.8 | all-reduce | flops 4 | bytes 32
  430.9 13.2 %all_gather.6 = s32[1,1,4,768]{3,1,0,2:T(1,128)S(1)} all-gather(s32[1,1,1,768]{3,1,0,2:T(1,128)S(1)} %bitcast.39), channel_id=1, replica_groups=mesh['groups'=2,'spec'=4,'band'=2,'sub'=2] {'spec'}, dimensions={2}, use_global_device_ids=true | all-gather | bytes 15360 | tf_op jit(solution)/shard_map/all_gather | solution.py:142
  444.6 4.8 copy.29
  449.4 7.5 %copy.21 = f32[432,4,1,1024]{3,1,0,2:T(4,128)} copy(f32[432,4,1,1024]{3,0,1,2:T(8,128)S(1)} %bitcast.36) | data formatting | bytes 14155776 | tf_op jit(solution)/shard_map/all_to_all | solution.py:171
  456.9 9.6 %reshape.434 = f32[432,16,256]{2,1,0:T(8,128)} reshape(f32[432,4,1,1024]{3,1,0,2:T(4,128)} %copy.21) | data formatting | bytes 14155776 | tf_op jit(solution)/shard_map/reshape | solution.py:174
  466.5 3.7 fusion.47
  470.2 3.2 collective-permute-start
  473.4 1.5 collective-permute-start.1
  475.1 4.1 collective-permute-done
  479.1 4.4 collective-permute-done.1
  483.6 4.6 pad_maximum_fusion
  488.2 5.8 %fusion.46 = (f32[432,18,1]{2,1,0:T(8,128)}, f32[432,18,1]{2,1,0:T(8,128)}) fusion(f32[432,18,256]{2,1,0:T(8,128)S(1)} %pad_maximum_fusion), kind=kLoop, calls=%fused_computation.111 | loop fusion | bytes 124416 | tf_op jit(solution)/shard_map/slice | solution.py:33
  494.0 4.2 copy.24
  498.3 4.2 copy.26
  502.5 0.6 collective-permute-start.3
  503.1 11.8 %scatter_custom_fusion.1 = f32[4096]{0:T(1024)S(1)} fusion(s32[3072]{0:T(1024)S(1)} %reshape.449, f32[3072]{0:T(1024)S(1)} %reshape.451, f32[]{:T(128)} %constant.37.clone.1), kind=kCustom, calls=%fused_computation.67 | custom fusion | bytes 16388
  515.2 3.9 copy.25
  519.1 4.0 copy.27
  523.1 26.8 %fusion.4 = f32[432,16,256]{2,1,0:T(8,128)} fusion(f32[432,16,256]{2,1,0:T(8,128)} %reshape.434, f32[432,1,256]{2,1,0:T(1,128)S(1)} %collective-permute-done, f32[432,1,256]{2,1,0:T(1,128)S(1)} %collective-permute-done.1, f32[432,18,1]{2,1,0:T(8,128)} %copy.27, f32[432,18,1]{2,1,0:T(8,128)} %copy.25, f32[16,256]{1,0:T(8,128)S(1)} %mul.608, ...), kind=kLoop, calls=%fused_computation.8 | loop fusion | flops 44236800 | bytes 15177856 | tf_op jit(solution)/shard_map/mul | solution.py:186
  (56 shorter events, 1.3 us)
Async XLA Ops:
  0.0 33.9 %copy-start = (f32[16,48]{1,0:T(8,128)S(1)}, f32[16,48]{1,0:T(8,128)}, u32[]{:S(2)}) copy-start(f32[16,48]{1,0:T(8,128)} %param.13) | copy-start | bytes 9220
  19.7 7.3 %copy-start.5 = (s32[1,1,1,1024]{3,2,1,0:T(1,128)S(1)}, s32[1,1,1,1024]{3,2,1,0:T(1,128)}, u32[]{:S(2)}) copy-start(s32[1,1,1,1024]{3,2,1,0:T(1,128)} %param.11) | copy-start | bytes 12292
  19.7 8.0 %copy-start.2 = (s32[1,1,1,768]{3,2,1,0:T(1,128)S(1)}, s32[1,1,1,768]{3,2,1,0:T(1,128)}, u32[]{:S(2)}) copy-start(s32[1,1,1,768]{3,2,1,0:T(1,128)} %param.14) | copy-start | bytes 9220
  19.7 12.1 %copy-start.6 = (f32[1,1,1,1024]{3,2,1,0:T(1,128)S(1)}, f32[1,1,1,1024]{3,2,1,0:T(1,128)}, u32[]{:S(2)}) copy-start(f32[1,1,1,1024]{3,2,1,0:T(1,128)} %param.10) | copy-start | bytes 12292
  19.7 13.5 %copy-start.3 = (f32[1,1,1,1024]{3,2,1,0:T(1,128)S(1)}, f32[1,1,1,1024]{3,2,1,0:T(1,128)}, u32[]{:S(2)}) copy-start(f32[1,1,1,1024]{3,2,1,0:T(1,128)} %param.9) | copy-start | bytes 12292
  19.7 14.2 %copy-start.4 = (s32[1,1,1,1024]{3,2,1,0:T(1,128)S(1)}, s32[1,1,1,1024]{3,2,1,0:T(1,128)}, u32[]{:S(2)}) copy-start(s32[1,1,1,1024]{3,2,1,0:T(1,128)} %param.12) | copy-start | bytes 12292
  19.7 162.2 %all-to-all-start = ((f32[432,4,1024]{2,0,1:T(8,128)}), f32[432,4,1024]{2,0,1:T(8,128)}, u32[]{:S(2)}, u32[]{:S(2)}) async-start(f32[432,4,1024]{2,0,1:T(8,128)} %copy.19), calls=%async_computation | async-start | bytes 14155776 | tf_op jit(solution)/shard_map/all_to_all | solution.py:160
  270.5 5.6 %copy-start.9 = (u32[32]{0:T(128)S(1)}, u32[32]{0:T(128)}, u32[]{:S(2)}) copy-start(u32[32]{0:T(128)} %constant.150) | copy-start | bytes 388
  270.5 173.8 %copy-start.8 = (s32[2]{0:T(128)S(1)}, s32[2]{0:T(128)}, u32[]{:S(2)}) copy-start(s32[2]{0:T(128)} %constant.140) | copy-start | bytes 28
  270.5 173.9 %copy-start.7 = (s32[2]{0:T(128)S(1)}, s32[2]{0:T(128)}, u32[]{:S(2)}) copy-start(s32[2]{0:T(128)} %constant.143) | copy-start | bytes 28
  270.5 174.1 %all-to-all-start.1 = ((f32[1728,1,1024]{2,1,0:T(1,128)}), f32[1728,1,1024]{2,1,0:T(1,128)}, u32[]{:S(2)}, u32[]{:S(2)}) async-start(f32[1728,1,1024]{2,1,0:T(1,128)} %copy.20), calls=%async_computation.1 | async-start | bytes 14155776 | tf_op jit(solution)/shard_map/all_to_all | solution.py:171
  470.2 9.0 %collective-permute-start = (f32[432,1,256]{2,1,0:T(1,128)S(1)}, f32[432,1,256]{2,1,0:T(1,128)S(1)}, u32[]{:S(2)}, u32[]{:S(2)}) collective-permute-start(f32[432,1,256]{2,1,0:T(1,128)S(1)} %get-tuple-element.14), channel_id=1, source_target_pairs={{0,2},{1,3},{4,6},{5,7},{8,10},{9,11},{12,14},{13,15},{16,18},{17,... | collective-permute-start | bytes 1327112 | tf_op jit(solution)/shard_map/ppermute | solution.py:30
  473.4 10.2 %collective-permute-start.1 = (f32[432,1,256]{2,1,0:T(1,128)S(1)}, f32[432,1,256]{2,1,0:T(1,128)S(1)}, u32[]{:S(2)}, u32[]{:S(2)}) collective-permute-start(f32[432,1,256]{2,1,0:T(1,128)S(1)} %get-tuple-element.13), channel_id=1, source_target_pairs={{2,0},{3,1},{6,4},{7,5},{10,8},{11,9},{14,12},{15,13},{18,16},{19,... | collective-permute-start | bytes 1327112 | tf_op jit(solution)/shard_map/ppermute | solution.py:33
  498.2 17.0 %collective-permute-start.2 = (f32[432,18,1]{0,2,1:T(1,128)S(1)}, f32[432,18,1]{0,2,1:T(1,128)S(1)}, u32[]{:S(2)}, u32[]{:S(2)}) collective-permute-start(f32[432,18,1]{0,2,1:T(1,128)S(1)} %copy.24), channel_id=1, source_target_pairs={{1,0},{0,1},{3,2},{2,3},{5,4},{4,5},{7,6},{6,7},{9,8},{8,9},{11,10... | collective-permute-start | bytes 93320 | tf_op jit(solution)/shard_map/ppermute | solution.py:33
  502.5 16.6 %collective-permute-start.3 = (f32[432,18,1]{0,2,1:T(1,128)S(1)}, f32[432,18,1]{0,2,1:T(1,128)S(1)}, u32[]{:S(2)}, u32[]{:S(2)}) collective-permute-start(f32[432,18,1]{0,2,1:T(1,128)S(1)} %copy.26), channel_id=1, source_target_pairs={{0,1},{1,0},{2,3},{3,2},{4,5},{5,4},{6,7},{7,6},{8,9},{9,8},{10,11... | collective-permute-start | bytes 93320 | tf_op jit(solution)/shard_map/ppermute | solution.py:30
  523.1 26.8 %copy-start.1 = (f32[16,48]{1,0:T(8,128)S(1)}, f32[16,48]{1,0:T(8,128)}, u32[]{:S(2)}) copy-start(f32[16,48]{1,0:T(8,128)} %param.13) | copy-start | bytes 9220
where the time goes:
time: 559 us; the launch traced here: 550 us
  blocking collectives  167 us (30%)
  waiting for transfers between devices  156 us (28%)
  local copies, waits for them, and re-layouts  142 us (25%)
  other arithmetic  66.7 us (12%)
  starting transfers between devices  17.4 us (3%)
    unnamed x1, blocking collectives  154 us
    all_to_all x1, waiting for transfers between devices, body(): lax.all_to_all(blocks, 'spec', split_axis=1, concat_axis=0, tiled=True)  147 us
    slice x12, local copies, waits for them, and re-layouts, shifted(): rolled = jnp.roll(values, dir_turn, axis=0)  42.8 us
    mul x1, other arithmetic, body(): return moved * sea_prop.reshape(rows, cols)[None]  26.8 us
    reshape x2, local copies, waits for them, and re-layouts, body(): blocks = spectrum.reshape(local_comps, spec_size, block_len)  19.7 us
    unnamed x26, local copies, waits for them, and re-layouts  17.9 us
    reshape x1, local copies, waits for them, and re-layouts, body(): sourced.reshape(ND * NF, 1, block_len)  13.8 us
    slice x3, local copies, waits for them, and re-layouts, with_halo(): lax.slice_in_dim(block, 0, width, axis=dim)  13.7 us
  transfers between devices with their start and end apart: 6, of which 3 were waited for; matrix products, arithmetic and copies ran while one was open for 5% of the time, Pallas kernels for 0%

commit v1 on v0

--- a/solution.py
+++ b/solution.py
@@ -1,8 +1,13 @@
 import math
+
+import functools
 
 import jax
 import jax.numpy as jnp
+import numpy as np
 from jax import lax
+from jax.experimental import pallas as pl
+from jax.experimental.pallas import tpu as pltpu
 from jax.sharding import PartitionSpec as P
 
 ND = 36
@@ -186,9 +191,395 @@
     return moved * sea_prop.reshape(rows, cols)[None]
 
 
+REACH = 4
+PAD = 7
+MESH = pl.DeviceIdType.MESH
+UNIT = (growth_ratio - 1.0 / growth_ratio) * 0.5 * (2.0 * math.pi / ND)
+
+
+def frequency_table():
+    n = np.arange(-PAD, NF + PAD, dtype=np.float64)
+    f = low_frequency * growth_ratio**n
+    last = low_frequency * growth_ratio ** (NF - 1)
+    rows = [
+        f,
+        f * (2.0 * math.pi / gravity),
+        quad_coef * (f / last) ** 2,
+        1.0 - np.exp(-ice_rate * (f / last) ** 2),
+        low_frequency / f,
+    ]
+    return np.stack(rows).astype(np.float32)
+
+
+def direction_table():
+    theta = 2.0 * math.pi * np.arange(ND) / ND
+    return np.stack([np.cos(theta), np.sin(theta)]).astype(np.float32)
+
+
+def quad(f, a, b):
+    return f * (f * (a * (1 / 2.4414) + b * (1 / 0.3164)) - (a * b) * (2.0 / 0.7725))
+
+
+def wave_kernel(
+    sizes,
+    f_hbm, aux_ref, slots_ref, count_ref, table_ref, freq_ref, dir_ref, out_hbm,
+    fx, g, ob, rows_out, rows_in, cols_in, aux_all, sums, fld, fric, wind,
+    load_sem, halo_send, halo_recv, aux_send, aux_recv, sum_send, sum_recv,
+    row_send, row_recv, col_send, col_recv, out_sem,
+):
+    own, nspec, nrow, ncol, most, total_rows = sizes
+    me = lax.axis_index("spec")
+    band = lax.axis_index("band")
+    sub = lax.axis_index("sub")
+    half = ncol // 2
+    blk_rows = nrow // nspec
+    xpos = (me == 0) | (me == nspec - 1)
+    ypos = me < nspec // 2
+    nxt, prv = lax.rem(me + 1, nspec), lax.rem(me + nspec - 1, nspec)
+
+    load = pltpu.make_async_copy(
+        f_hbm, fx.at[pl.ds(REACH, own), pl.ds(PAD, NF)], load_sem
+    )
+    load.start()
+    barrier = pltpu.get_barrier_semaphore()
+    for o in range(1, nspec):
+        pl.semaphore_signal(
+            barrier, inc=1, device_id={"spec": lax.rem(me + o, nspec)}, device_id_type=MESH
+        )
+    pl.semaphore_signal(barrier, inc=1, device_id={"band": 1 - band}, device_id_type=MESH)
+    pl.semaphore_signal(barrier, inc=1, device_id={"sub": 1 - sub}, device_id_type=MESH)
+    zero = jnp.zeros((nrow, ncol), jnp.float32)
+
+    def clear(d, _):
+        for m in range(PAD):
+            fx[d, m] = zero
+            fx[d, PAD + NF + m] = zero
+        return 0
+
+    lax.fori_loop(0, own + 2 * REACH, clear, 0)
+    pl.semaphore_wait(barrier, nspec + 1)
+
+    lows, highs = [], []
+    for k in range(REACH):
+        lows.append(
+            pltpu.make_async_remote_copy(
+                src_ref=f_hbm.at[own - 1 - k],
+                dst_ref=fx.at[REACH - 1 - k, pl.ds(PAD, NF)],
+                send_sem=halo_send.at[k],
+                recv_sem=halo_recv.at[k],
+                device_id={"spec": nxt},
+                device_id_type=MESH,
+            )
+        )
+        highs.append(
+            pltpu.make_async_remote_copy(
+                src_ref=f_hbm.at[k],
+                dst_ref=fx.at[REACH + own + k, pl.ds(PAD, NF)],
+                send_sem=halo_send.at[REACH + k],
+                recv_sem=halo_recv.at[REACH + k],
+                device_id={"spec": prv},
+                device_id_type=MESH,
+            )
+        )
+    for k in range(REACH):
+        lows[k].start()
+        highs[k].start()
+
+    place = (
+        lax.broadcasted_iota(jnp.int32, (blk_rows, ncol), 0) * ncol
+        + lax.broadcasted_iota(jnp.int32, (blk_rows, ncol), 1)
+    )
+    count = count_ref[0]
+
+    def mark(i, flags):
+        for j in range(16):
+            m = i * 16 + j
+            slot = jnp.where(m < count, slots_ref[m], -1)
+            flags = jnp.where(place == slot, 1.0, flags)
+        return flags
+
+    flags = lax.fori_loop(0, most // 16, mark, jnp.zeros((blk_rows, ncol), jnp.float32))
+    n_aux = 4 * blk_rows
+    aux_all[me, pl.ds(0, n_aux)] = aux_ref[...]
+    for i in range(blk_rows):
+        aux_all[me, n_aux + i] = flags[i : i + 1, :]
+
+    def exchange(buffer, send, recv):
+        return [
+            pltpu.make_async_remote_copy(
+                src_ref=buffer.at[me],
+                dst_ref=buffer.at[me],
+                send_sem=send.at[o - 1],
+                recv_sem=recv.at[o - 1],
+                device_id={"spec": lax.rem(me + o, nspec)},
+                device_id_type=MESH,
+            )
+            for o in range(1, nspec)
+        ]
+
+    def arrivals(buffer, send, recv):
+        for o in range(1, nspec):
+            pltpu.make_async_remote_copy(
+                src_ref=buffer.at[me],
+                dst_ref=buffer.at[lax.rem(me + nspec - o, nspec)],
+                send_sem=send.at[o - 1],
+                recv_sem=recv.at[o - 1],
+                device_id={"spec": lax.rem(me + o, nspec)},
+                device_id_type=MESH,
+            ).wait_recv()
+
+    aux_sends = exchange(aux_all, aux_send, aux_recv)
+    for c in aux_sends:
+        c.start()
+
+    load.wait()
+
+    def add_up(n, carry):
+        energy, inverse = carry
+        part = fx[REACH, PAD + n]
+        for d in range(1, own):
+            part = part + fx[REACH + d, PAD + n]
+        return energy + part * freq_ref[0, PAD + n], inverse + part
+
+    energy, inverse = lax.fori_loop(0, NF, add_up, (zero, zero))
+    sums[me, 0] = energy
+    sums[me, 1] = inverse
+    sum_sends = exchange(sums, sum_send, sum_recv)
+    for c in sum_sends:
+        c.start()
+
+    arrivals(aux_all, aux_send, aux_recv)
+    for p in range(nspec):
+        for f in range(5):
+            for i in range(blk_rows):
+                r = p * blk_rows + i
+                fld[f, r : r + 1, :] = aux_all[p, f * blk_rows + i]
+    depth = fld[3]
+
+    def rub(n, _):
+        value = zero
+        for c in range(table_ref.shape[0]):
+            value = jnp.where(depth == float(c), table_ref[c, n], value)
+        fric[n] = value
+        return 0
+
+    lax.fori_loop(0, NF, rub, 0)
+
+    arrivals(sums, sum_send, sum_recv)
+    energy = sums[0, 0]
+    inverse = sums[0, 1]
+    for p in range(1, nspec):
+        energy = energy + sums[p, 0]
+        inverse = inverse + sums[p, 1]
+    mean_freq = energy / inverse
+    energy = energy * UNIT
+    mean_wave = mean_freq * mean_freq * (4.0 * math.pi**2 / gravity)
+    steep = energy * mean_wave * mean_wave * (1.0 / steep_ref)
+    speed, wdir, ice, sea = fld[0], fld[1], fld[2], fld[4]
+    open_water = 1.0 - ice
+    row = lax.broadcasted_iota(jnp.int32, (nrow, ncol), 0)
+    lane = lax.broadcasted_iota(jnp.int32, (nrow, ncol), 1)
+    lat = latitudes((row + band * nrow).astype(jnp.float32), total_rows)
+    fld[0] = speed * jnp.cos(wdir)
+    fld[1] = speed * jnp.sin(wdir)
+    fld[2] = sea * ice
+    fld[3] = (dissip_coef * steep * steep / mean_freq) * open_water
+    fld[5] = wind_coef * open_water
+    fld[6] = courant_limit / jnp.cos(lat)
+
+    def source(d):
+        t = me * own + d
+        wind[...] = fld[0] * dir_ref[0, t] + fld[1] * dir_ref[1, t]
+
+        def one(n, _):
+            for h in range(nrow // 8):
+                rs = pl.ds(8 * h, 8)
+
+                def F(dd, m):
+                    return fx[REACH + d + dd, PAD + m + n, rs, :]
+
+                c = F(0, 0)
+                here = quad(c, F(1, 3), F(-3, -4)) + quad(c, F(-1, 3), F(3, -4))
+                down = quad(F(-1, -3), c, F(-4, -7)) + quad(F(1, -3), c, F(4, -7))
+                up = quad(F(3, 4), F(4, 7), c) + quad(F(-3, 4), F(-4, 7), c)
+                transfer = (
+                    here * (-2.0 * freq_ref[2, PAD + n])
+                    + down * freq_ref[2, PAD + n - 3]
+                    + up * freq_ref[2, PAD + n + 4]
+                )
+                growth = jnp.maximum(wind[rs, :] * freq_ref[1, PAD + n] - 1.0, 0.0) * fld[5, rs, :]
+                rate = growth - fld[3, rs, :] * freq_ref[0, PAD + n] - fric[n, rs, :]
+                value = jnp.maximum(c * (1.0 + rate) + transfer, 0.0)
+                value = value * (fld[4, rs, :] - fld[2, rs, :] * freq_ref[3, PAD + n])
+                g[d, n, rs, :] = value
+            rows_out[d, n] = jnp.where(ypos, g[d, n, nrow - 1 : nrow, :], g[d, n, 0:1, :])
+            return 0
+
+        lax.fori_loop(0, NF, one, 0)
+
+    def edges(d):
+        side = pl.multiple_of(xpos.astype(jnp.int32) * half, half)
+        return [
+            pltpu.make_async_remote_copy(
+                src_ref=rows_out.at[d],
+                dst_ref=rows_in.at[d],
+                send_sem=row_send.at[d],
+                recv_sem=row_recv.at[d],
+                device_id={"band": 1 - band},
+                device_id_type=MESH,
+            ),
+            pltpu.make_async_remote_copy(
+                src_ref=g.at[d, :, :, pl.ds(side, half)],
+                dst_ref=cols_in.at[d],
+                send_sem=col_send.at[d],
+                recv_sem=col_recv.at[d],
+                device_id={"sub": 1 - sub},
+                device_id_type=MESH,
+            ),
+        ]
+
+    bands = lax.axis_size("band")
+    inside = jnp.where(ypos, band > 0, band < bands - 1).astype(jnp.float32)
+
+    def advance(d):
+        t = me * own + d
+        cos_d = jnp.abs(dir_ref[0, t])
+        sin_d = jnp.abs(dir_ref[1, t]) * courant_limit
+
+        def one(n, _):
+            c = g[d, n]
+            e = cols_in[d, n]
+            wide = jnp.concatenate([e, e], axis=1)
+            west = jnp.where(lane == 0, pltpu.roll(wide, 1, 1), pltpu.roll(c, 1, 1))
+            east = jnp.where(
+                lane == ncol - 1, pltpu.roll(wide, ncol - 1, 1), pltpu.roll(c, ncol - 1, 1)
+            )
+            far = rows_in[d, n] * inside
+            south = jnp.where(row == 0, far, pltpu.roll(c, 1, 0))
+            north = jnp.where(row == nrow - 1, far, pltpu.roll(c, nrow - 1, 0))
+            gx = jnp.where(xpos, west, east)
+            gy = jnp.where(ypos, south, north)
+            ratio = freq_ref[4, PAD + n]
+            moved = c - (fld[6] * (ratio * cos_d)) * (c - gx) - (ratio * sin_d) * (c - gy)
+            ob[d, n] = moved * fld[4]
+            return 0
+
+        lax.fori_loop(0, NF, one, 0)
+        copy = pltpu.make_async_copy(ob.at[d], out_hbm.at[d], out_sem.at[d])
+        copy.start()
+        return copy
+
+    mid = own // 2
+    order = [mid]
+    for k in range(1, mid + 1):
+        order += [mid - k, mid + k]
+    pending = None
+    started, outs = [], []
+    for d in order:
+        if d < mid:
+            lows[mid - d - 1].wait_recv()
+        elif d > mid:
+            highs[d - mid - 1].wait_recv()
+        source(d)
+        now = edges(d)
+        for c in now:
+            c.start()
+        started += now
+        if pending is not None:
+            for c in pending[1]:
+                c.wait_recv()
+            outs.append(advance(pending[0]))
+        pending = (d, now)
+    for c in pending[1]:
+        c.wait_recv()
+    outs.append(advance(pending[0]))
+    for c in started + lows + highs + aux_sends + sum_sends:
+        c.wait_send()
+    for c in outs:
+        c.wait()
+
+
+def halo_body(spectrum, wind_speed, wind_dir, ice_mask, depth_class, bottom_table, sea_slots, sea_count):
+    comps, nrow, ncol = spectrum.shape
+    nspec = lax.axis_size("spec")
+    own = comps // NF
+    most = sea_slots.shape[-1]
+    blk_rows = nrow // nspec
+    total_rows = nrow * lax.axis_size("band")
+    aux = jnp.stack(
+        [
+            wind_speed.reshape(blk_rows, 1, ncol),
+            wind_dir.reshape(blk_rows, 1, ncol),
+            ice_mask.reshape(blk_rows, 1, ncol).astype(jnp.float32),
+            depth_class.reshape(blk_rows, 1, ncol).astype(jnp.float32),
+        ]
+    ).reshape(4 * blk_rows, 1, ncol)
+    f32 = jnp.float32
+    hbm = pl.BlockSpec(memory_space=pl.ANY)
+    vmem = pl.BlockSpec(memory_space=pltpu.VMEM)
+    smem = pl.BlockSpec(memory_space=pltpu.SMEM)
+    dma = pltpu.SemaphoreType.DMA
+    moved = pl.pallas_call(
+        functools.partial(wave_kernel, (own, nspec, nrow, ncol, most, total_rows)),
+        out_shape=jax.ShapeDtypeStruct((own, NF, nrow, ncol), f32),
+        in_specs=[hbm, vmem, smem, smem, smem, smem, smem],
+        out_specs=hbm,
+        scratch_shapes=[
+            pltpu.VMEM((own + 2 * REACH, NF + 2 * PAD, nrow, ncol), f32),
+            pltpu.VMEM((own, NF, nrow, ncol), f32),
+            pltpu.VMEM((own, NF, nrow, ncol), f32),
+            pltpu.VMEM((own, NF, 1, ncol), f32),
+            pltpu.VMEM((own, NF, 1, ncol), f32),
+            pltpu.VMEM((own, NF, nrow, ncol // 2), f32),
+            pltpu.VMEM((nspec, 5 * blk_rows, 1, ncol), f32),
+            pltpu.VMEM((nspec, 2, nrow, ncol), f32),
+            pltpu.VMEM((7, nrow, ncol), f32),
+            pltpu.VMEM((NF, nrow, ncol), f32),
+            pltpu.VMEM((nrow, ncol), f32),
+            dma,
+            dma((2 * REACH,)),
+            dma((2 * REACH,)),
+            dma((nspec - 1,)),
+            dma((nspec - 1,)),
+            dma((nspec - 1,)),
+            dma((nspec - 1,)),
+            dma((own,)),
+            dma((own,)),
+            dma((own,)),
+            dma((own,)),
+            dma((own,)),
+        ],
+        compiler_params=pltpu.CompilerParams(
+            collective_id=0, has_side_effects=True, vmem_limit_bytes=56 * 2**20
+        ),
+    )(
+        spectrum.reshape(own, NF, nrow, ncol),
+        aux,
+        sea_slots.reshape(most),
+        sea_count.reshape(1),
+        bottom_table,
+        jnp.asarray(frequency_table()),
+        jnp.asarray(direction_table()),
+    )
+    return moved.reshape(comps, nrow, ncol)
+
+
+def step(shape, spectrum, *rest):
+    comps, nrow, ncol = spectrum.shape
+    fits = (
+        shape["spec"] == 4
+        and comps * 4 == ND * NF
+        and shape["band"] == 2
+        and shape["sub"] == 2
+        and nrow % 8 == 0
+        and ncol % 256 == 0
+    )
+    return (halo_body if fits else body)(spectrum, *rest)
+
+
 def solution(mesh):
     return jax.shard_map(
-        body,
+        functools.partial(step, dict(mesh.shape)),
         mesh=mesh,
         in_specs=(
             P(("groups", "spec"), "band", "sub"),

time: 559 us -> 221 us (0.40); the launches traced: 550 us -> 220 us
  Pallas kernels: 0 us -> 209 us
  blocking collectives: 167 us -> 0 us
  waiting for transfers between devices: 156 us -> 0 us
  local copies, waits for them, and re-layouts: 142 us -> 6.78 us
  other arithmetic: 66.7 us -> 3.99 us
  starting transfers between devices: 17.4 us -> 0 us
    pallas_call x0 -> x1, Pallas kernels: none -> 209 us  [halo_body(): pl.pallas_call(functools.partial(wave_kernel, (own, nspec, nrow, ncol, mo...]
    unnamed x1 -> x0, blocking collectives: 154 us -> none
    all_to_all x2 -> x0, waiting for transfers between devices: 147 us -> none  [the longest x1 147 us: body(): lax.all_to_all(blocks, 'spec', split_axis=1, concat_axis=0, tiled=True)]
    slice x17 -> x0, local copies, waits for them, and re-layouts: 61.3 us -> none  [the longest x12 42.8 us: shifted(): rolled = jnp.roll(values, dir_turn, axis=0)]
    mul x12 -> x0, other arithmetic: 55.4 us -> none  [the longest x1 26.8 us: body(): return moved * sea_prop.reshape(rows, cols)[None]]
    reshape x4 -> x0, local copies, waits for them, and re-layouts: 43.1 us -> none  [the longest x2 19.7 us: body(): blocks = spectrum.reshape(local_comps, spec_size, block_len)]
    all_gather x1 -> x0, blocking collectives: 13.2 us -> none  [body(): lax.all_gather(sea_slots, 'spec', axis=2, tiled=True)]
    all_to_all x2 -> x0, starting transfers between devices: 12 us -> none  [the longest x1 6.46 us: body(): lax.all_to_all(blocks, 'spec', split_axis=1, concat_axis=0, tiled=True)]
  transfers between devices with their start and end apart: 6 -> 0, of which waited for: 3 -> 0; matrix products, arithmetic and copies ran while one was open for 5% -> 0% of each run, Pallas kernels for 0% -> 0%
where the time goes in v1:
time: 221 us; the launch traced here: 220 us
  Pallas kernels  209 us (95%)
  local copies, waits for them, and re-layouts  6.78 us (3%)
  other arithmetic  3.99 us (2%)
    pallas_call x1, Pallas kernels, halo_body(): pl.pallas_call(functools.partial(wave_kernel, (own, nspec, nrow, ncol, mo...  209 us
    unnamed x1, local copies, waits for them, and re-layouts  6.78 us

profile of v1, /device:TPU:0, one launch (start us, length us, event | category | flops | bytes accessed | tf_op | source)
XLA Modules:
  0.0 220.3 jit_solution(13896328120550664833)
XLA Ops:
  0.7 0.7 convert_element_type.30
  1.3 0.7 convert_element_type.32
  2.0 1.3 reduce.slots_ref
  3.3 1.3 pad_maximum_fusion
  4.6 208.8 %shard_map.100 = f32[9,48,16,256]{3,2,1,0:T(8,128)} custom-call(f32[9,48,16,256]{3,2,1,0:T(8,128)} %bitcast.10, f32[16,1,256]{2,1,0:T(1,128)} %bitcast.11, s32[768]{0:T(1024)} %reduce.slots_ref, s32[1]{0:T(128)} %bitcast.8.count_ref, f32[16,48]{1,0:T(8,128)} %table_ref.1, f32[5,62]{1,0:T(8,128)} %constant.4.clone.freq_ref, f32[2,36]{1,0:T(2,128)} %constant.5.clone.dir_ref), custom_call_target="tpu_custom_call" | custom-call | tf_op jit(solution)/shard_map/pallas_call | solution.py:522
  213.5 6.8 %copy.17 = f32[432,16,256]{2,1,0:T(8,128)} copy(f32[432,16,256]{2,1,0:T(8,128)} %bitcast.9) | data formatting | bytes 14155776

commit v2 on v1

--- a/solution.py
+++ b/solution.py
@@ -281,9 +281,8 @@
                 device_id_type=MESH,
             )
         )
-    for k in range(REACH):
-        lows[k].start()
-        highs[k].start()
+    lows[0].start()
+    highs[0].start()
 
     place = (
         lax.broadcasted_iota(jnp.int32, (blk_rows, ncol), 0) * ncol
@@ -347,6 +346,8 @@
     sum_sends = exchange(sums, sum_send, sum_recv)
     for c in sum_sends:
         c.start()
+    lows[1].start()
+    highs[1].start()
 
     arrivals(aux_all, aux_send, aux_recv)
     for p in range(nspec):
@@ -378,7 +379,6 @@
     speed, wdir, ice, sea = fld[0], fld[1], fld[2], fld[4]
     open_water = 1.0 - ice
     row = lax.broadcasted_iota(jnp.int32, (nrow, ncol), 0)
-    lane = lax.broadcasted_iota(jnp.int32, (nrow, ncol), 1)
     lat = latitudes((row + band * nrow).astype(jnp.float32), total_rows)
     fld[0] = speed * jnp.cos(wdir)
     fld[1] = speed * jnp.sin(wdir)
@@ -441,30 +441,49 @@
     bands = lax.axis_size("band")
     inside = jnp.where(ypos, band > 0, band < bands - 1).astype(jnp.float32)
 
+    xshift = jnp.where(xpos, 1, half - 1)
+    yshift = jnp.where(ypos, 1, 7)
+    nt = nrow // 8
+    lane = lax.broadcasted_iota(jnp.int32, (nrow, half), 1)
+    tier = lax.broadcasted_iota(jnp.int32, (8, ncol), 0)
+    xlow = lane == jnp.where(xpos, 0, -1)
+    xhigh = lane == jnp.where(xpos, -1, half - 1)
+    ylow = tier == jnp.where(ypos, 0, -1)
+    yhigh = tier == jnp.where(ypos, -1, 7)
+
     def advance(d):
         t = me * own + d
         cos_d = jnp.abs(dir_ref[0, t])
         sin_d = jnp.abs(dir_ref[1, t]) * courant_limit
 
-        def one(n, _):
-            c = g[d, n]
-            e = cols_in[d, n]
-            wide = jnp.concatenate([e, e], axis=1)
-            west = jnp.where(lane == 0, pltpu.roll(wide, 1, 1), pltpu.roll(c, 1, 1))
-            east = jnp.where(
-                lane == ncol - 1, pltpu.roll(wide, ncol - 1, 1), pltpu.roll(c, ncol - 1, 1)
-            )
-            far = rows_in[d, n] * inside
-            south = jnp.where(row == 0, far, pltpu.roll(c, 1, 0))
-            north = jnp.where(row == nrow - 1, far, pltpu.roll(c, nrow - 1, 0))
-            gx = jnp.where(xpos, west, east)
-            gy = jnp.where(ypos, south, north)
-            ratio = freq_ref[4, PAD + n]
-            moved = c - (fld[6] * (ratio * cos_d)) * (c - gx) - (ratio * sin_d) * (c - gy)
-            ob[d, n] = moved * fld[4]
+        def one(i, _):
+            for j in range(4):
+                n = i * 4 + j
+                c = g[d, n]
+                e = pltpu.roll(cols_in[d, n], xshift, 1)
+                r0 = pltpu.roll(c[:, :half], xshift, 1)
+                r1 = pltpu.roll(c[:, half:], xshift, 1)
+                gx = jnp.concatenate(
+                    [
+                        jnp.where(xlow, e, jnp.where(xhigh, r1, r0)),
+                        jnp.where(xhigh, e, jnp.where(xlow, r0, r1)),
+                    ],
+                    axis=1,
+                )
+                far = rows_in[d, n] * inside
+                tiles = [pltpu.roll(c[8 * k : 8 * k + 8], yshift, 0) for k in range(nt)]
+                parts = []
+                for k in range(nt):
+                    below = tiles[k - 1] if k > 0 else far
+                    above = tiles[k + 1] if k < nt - 1 else far
+                    parts.append(jnp.where(ylow, below, jnp.where(yhigh, above, tiles[k])))
+                gy = jnp.concatenate(parts, axis=0)
+                ratio = freq_ref[4, PAD + n]
+                moved = c - (fld[6] * (ratio * cos_d)) * (c - gx) - (ratio * sin_d) * (c - gy)
+                ob[d, n] = moved * fld[4]
             return 0
 
-        lax.fori_loop(0, NF, one, 0)
+        lax.fori_loop(0, NF // 4, one, 0)
         copy = pltpu.make_async_copy(ob.at[d], out_hbm.at[d], out_sem.at[d])
         copy.start()
         return copy
@@ -477,7 +496,12 @@
     started, outs = [], []
     for d in order:
         if d < mid:
-            lows[mid - d - 1].wait_recv()
+            k = mid - d - 1
+            lows[k].wait_recv()
+            for side in (lows, highs):
+                side[k].wait_send()
+                if k + 2 < REACH:
+                    side[k + 2].start()
         elif d > mid:
             highs[d - mid - 1].wait_recv()
         source(d)
@@ -493,7 +517,7 @@
     for c in pending[1]:
         c.wait_recv()
     outs.append(advance(pending[0]))
-    for c in started + lows + highs + aux_sends + sum_sends:
+    for c in started + aux_sends + sum_sends:
         c.wait_send()
     for c in outs:
         c.wait()

time: 221 us -> 169 us (0.76)
  Pallas kernels: 209 us -> 157 us
    pallas_call x1, Pallas kernels: 209 us -> 157 us  [halo_body(): pl.pallas_call(functools.partial(wave_kernel, (own, nspec, nrow, ncol, mo...]
where the time goes in v2:
time: 169 us
  Pallas kernels  157 us (93%)
  local copies, waits for them, and re-layouts  6.78 us (4%)
  other arithmetic  3.99 us (2%)
    pallas_call x1, Pallas kernels, halo_body(): pl.pallas_call(functools.partial(wave_kernel, (own, nspec, nrow, ncol, mo...  157 us
    unnamed x1, local copies, waits for them, and re-layouts  6.78 us

profile of v2, /device:TPU:0, one launch (start us, length us, event | category | flops | bytes accessed | tf_op | source)
XLA Modules:
  0.0 168.8 jit_solution(11099156698813936790)
XLA Ops:
  0.7 0.7 convert_element_type.30
  1.3 0.7 convert_element_type.32
  2.0 1.3 reduce.slots_ref
  3.3 1.3 pad_maximum_fusion
  4.6 157.3 %shard_map.100 = f32[9,48,16,256]{3,2,1,0:T(8,128)} custom-call(f32[9,48,16,256]{3,2,1,0:T(8,128)} %bitcast.10, f32[16,1,256]{2,1,0:T(1,128)} %bitcast.11, s32[768]{0:T(1024)} %reduce.slots_ref, s32[1]{0:T(128)} %bitcast.8.count_ref, f32[16,48]{1,0:T(8,128)} %table_ref.1, f32[5,62]{1,0:T(8,128)} %constant.4.clone.freq_ref, f32[2,36]{1,0:T(2,128)} %constant.5.clone.dir_ref), custom_call_target="tpu_custom_call" | custom-call | tf_op jit(solution)/shard_map/pallas_call | solution.py:546
  162.0 6.8 %copy.17 = f32[432,16,256]{2,1,0:T(8,128)} copy(f32[432,16,256]{2,1,0:T(8,128)} %bitcast.9) | data formatting | bytes 14155776

commit v3 on v2

--- a/solution.py
+++ b/solution.py
@@ -192,6 +192,8 @@
 
 
 REACH = 4
+PIECES = 4
+DEPTH = 2
 PAD = 7
 MESH = pl.DeviceIdType.MESH
 UNIT = (growth_ratio - 1.0 / growth_ratio) * 0.5 * (2.0 * math.pi / ND)
@@ -222,7 +224,8 @@
 
 def wave_kernel(
     sizes,
-    f_hbm, aux_ref, slots_ref, count_ref, table_ref, freq_ref, dir_ref, out_hbm,
+    f_hbm, speed_in, dir_in, ice_in, depth_in, slots_in, count_in, table_in, freq_in, dir_tab, out_hbm,
+    speed_ref, dir_in_ref, ice_ref, depth_ref, slots_ref, count_ref, table_ref, freq_ref, dir_ref, small_sem,
     fx, g, ob, rows_out, rows_in, cols_in, aux_all, sums, fld, fric, wind,
     load_sem, halo_send, halo_recv, aux_send, aux_recv, sum_send, sum_recv,
     row_send, row_recv, col_send, col_recv, out_sem,
@@ -241,6 +244,24 @@
         f_hbm, fx.at[pl.ds(REACH, own), pl.ds(PAD, NF)], load_sem
     )
     load.start()
+    smalls = [
+        pltpu.make_async_copy(src, dst, small_sem.at[i])
+        for i, (src, dst) in enumerate(
+            (
+                (slots_in, slots_ref),
+                (count_in, count_ref),
+                (speed_in, speed_ref),
+                (dir_in, dir_in_ref),
+                (ice_in, ice_ref),
+                (depth_in, depth_ref),
+                (freq_in, freq_ref),
+                (table_in, table_ref),
+                (dir_tab, dir_ref),
+            )
+        )
+    ]
+    for c in smalls:
+        c.start()
     barrier = pltpu.get_barrier_semaphore()
     for o in range(1, nspec):
         pl.semaphore_signal(
@@ -259,48 +280,58 @@
     lax.fori_loop(0, own + 2 * REACH, clear, 0)
     pl.semaphore_wait(barrier, nspec + 1)
 
+    part = NF // PIECES
     lows, highs = [], []
     for k in range(REACH):
-        lows.append(
-            pltpu.make_async_remote_copy(
-                src_ref=f_hbm.at[own - 1 - k],
-                dst_ref=fx.at[REACH - 1 - k, pl.ds(PAD, NF)],
-                send_sem=halo_send.at[k],
-                recv_sem=halo_recv.at[k],
-                device_id={"spec": nxt},
-                device_id_type=MESH,
+        for q in range(PIECES):
+            at = k * PIECES + q
+            src, dst = pl.ds(q * part, part), pl.ds(PAD + q * part, part)
+            lows.append(
+                pltpu.make_async_remote_copy(
+                    src_ref=f_hbm.at[own - 1 - k, src],
+                    dst_ref=fx.at[REACH - 1 - k, dst],
+                    send_sem=halo_send.at[at],
+                    recv_sem=halo_recv.at[at],
+                    device_id={"spec": nxt},
+                    device_id_type=MESH,
+                )
             )
-        )
-        highs.append(
-            pltpu.make_async_remote_copy(
-                src_ref=f_hbm.at[k],
-                dst_ref=fx.at[REACH + own + k, pl.ds(PAD, NF)],
-                send_sem=halo_send.at[REACH + k],
-                recv_sem=halo_recv.at[REACH + k],
-                device_id={"spec": prv},
-                device_id_type=MESH,
+            highs.append(
+                pltpu.make_async_remote_copy(
+                    src_ref=f_hbm.at[k, src],
+                    dst_ref=fx.at[REACH + own + k, dst],
+                    send_sem=halo_send.at[REACH * PIECES + at],
+                    recv_sem=halo_recv.at[REACH * PIECES + at],
+                    device_id={"spec": prv},
+                    device_id_type=MESH,
+                )
             )
-        )
-    lows[0].start()
-    highs[0].start()
+    for at in range(DEPTH):
+        lows[at].start()
+        highs[at].start()
+
+    for c in smalls:
+        c.wait()
 
     place = (
         lax.broadcasted_iota(jnp.int32, (blk_rows, ncol), 0) * ncol
         + lax.broadcasted_iota(jnp.int32, (blk_rows, ncol), 1)
     )
-    count = count_ref[0]
+    count = count_ref[0, 0, 0, 0]
 
     def mark(i, flags):
         for j in range(16):
             m = i * 16 + j
-            slot = jnp.where(m < count, slots_ref[m], -1)
+            slot = jnp.where(m < count, slots_ref[0, 0, 0, m], -1)
             flags = jnp.where(place == slot, 1.0, flags)
         return flags
 
     flags = lax.fori_loop(0, most // 16, mark, jnp.zeros((blk_rows, ncol), jnp.float32))
     n_aux = 4 * blk_rows
-    aux_all[me, pl.ds(0, n_aux)] = aux_ref[...]
     for i in range(blk_rows):
+        for f, ref in enumerate((speed_ref, dir_in_ref, ice_ref, depth_ref)):
+            piece = ref[0, 0, 0:1, i * ncol : (i + 1) * ncol]
+            aux_all[me, f * blk_rows + i] = piece.astype(jnp.float32)
         aux_all[me, n_aux + i] = flags[i : i + 1, :]
 
     def exchange(buffer, send, recv):
@@ -346,8 +377,6 @@
     sum_sends = exchange(sums, sum_send, sum_recv)
     for c in sum_sends:
         c.start()
-    lows[1].start()
-    highs[1].start()
 
     arrivals(aux_all, aux_send, aux_recv)
     for p in range(nspec):
@@ -387,7 +416,7 @@
     fld[5] = wind_coef * open_water
     fld[6] = courant_limit / jnp.cos(lat)
 
-    def source(d):
+    def source(d, first, end):
         t = me * own + d
         wind[...] = fld[0] * dir_ref[0, t] + fld[1] * dir_ref[1, t]
 
@@ -415,7 +444,7 @@
             rows_out[d, n] = jnp.where(ypos, g[d, n, nrow - 1 : nrow, :], g[d, n, 0:1, :])
             return 0
 
-        lax.fori_loop(0, NF, one, 0)
+        lax.fori_loop(first, end, one, 0)
 
     def edges(d):
         side = pl.multiple_of(xpos.astype(jnp.int32) * half, half)
@@ -493,18 +522,30 @@
     for k in range(1, mid + 1):
         order += [mid - k, mid + k]
     pending = None
+    final = REACH * PIECES - 1
+    cut = NF - part - PAD
     started, outs = [], []
     for d in order:
+        first = 0
         if d < mid:
-            k = mid - d - 1
-            lows[k].wait_recv()
-            for side in (lows, highs):
-                side[k].wait_send()
-                if k + 2 < REACH:
-                    side[k + 2].start()
+            for at in range((mid - d - 1) * PIECES, (mid - d) * PIECES):
+                if at == final:
+                    for b in range(final + 1 - PIECES, final):
+                        highs[b].wait_recv()
+                    source(0, 0, cut)
+                    source(own - 1, 0, cut)
+                    first = cut
+                lows[at].wait_recv()
+                for side in (lows, highs):
+                    side[at].wait_send()
+                    if at + DEPTH < REACH * PIECES:
+                        side[at + DEPTH].start()
         elif d > mid:
-            highs[d - mid - 1].wait_recv()
-        source(d)
+            for at in range((d - mid - 1) * PIECES, (d - mid) * PIECES):
+                if d < own - 1 or at == final:
+                    highs[at].wait_recv()
+            first = cut if d == own - 1 else 0
+        source(d, first, NF)
         now = edges(d)
         for c in now:
             c.start()
@@ -530,25 +571,25 @@
     most = sea_slots.shape[-1]
     blk_rows = nrow // nspec
     total_rows = nrow * lax.axis_size("band")
-    aux = jnp.stack(
-        [
-            wind_speed.reshape(blk_rows, 1, ncol),
-            wind_dir.reshape(blk_rows, 1, ncol),
-            ice_mask.reshape(blk_rows, 1, ncol).astype(jnp.float32),
-            depth_class.reshape(blk_rows, 1, ncol).astype(jnp.float32),
-        ]
-    ).reshape(4 * blk_rows, 1, ncol)
     f32 = jnp.float32
     hbm = pl.BlockSpec(memory_space=pl.ANY)
-    vmem = pl.BlockSpec(memory_space=pltpu.VMEM)
-    smem = pl.BlockSpec(memory_space=pltpu.SMEM)
     dma = pltpu.SemaphoreType.DMA
     moved = pl.pallas_call(
         functools.partial(wave_kernel, (own, nspec, nrow, ncol, most, total_rows)),
         out_shape=jax.ShapeDtypeStruct((own, NF, nrow, ncol), f32),
-        in_specs=[hbm, vmem, smem, smem, smem, smem, smem],
+        in_specs=[hbm] * 10,
         out_specs=hbm,
         scratch_shapes=[
+            pltpu.VMEM(wind_speed.shape, f32),
+            pltpu.VMEM(wind_dir.shape, f32),
+            pltpu.VMEM(ice_mask.shape, jnp.int32),
+            pltpu.VMEM(depth_class.shape, jnp.int32),
+            pltpu.SMEM(sea_slots.shape, jnp.int32),
+            pltpu.SMEM(sea_count.shape, jnp.int32),
+            pltpu.SMEM(bottom_table.shape, f32),
+            pltpu.SMEM(frequency_table().shape, f32),
+            pltpu.SMEM(direction_table().shape, f32),
+            dma((9,)),
             pltpu.VMEM((own + 2 * REACH, NF + 2 * PAD, nrow, ncol), f32),
             pltpu.VMEM((own, NF, nrow, ncol), f32),
             pltpu.VMEM((own, NF, nrow, ncol), f32),
@@ -561,8 +602,8 @@
             pltpu.VMEM((NF, nrow, ncol), f32),
             pltpu.VMEM((nrow, ncol), f32),
             dma,
-            dma((2 * REACH,)),
-            dma((2 * REACH,)),
+            dma((2 * REACH * PIECES,)),
+            dma((2 * REACH * PIECES,)),
             dma((nspec - 1,)),
             dma((nspec - 1,)),
             dma((nspec - 1,)),
@@ -578,9 +619,12 @@
         ),
     )(
         spectrum.reshape(own, NF, nrow, ncol),
-        aux,
-        sea_slots.reshape(most),
-        sea_count.reshape(1),
+        wind_speed,
+        wind_dir,
+        ice_mask,
+        depth_class,
+        sea_slots,
+        sea_count,
         bottom_table,
         jnp.asarray(frequency_table()),
         jnp.asarray(direction_table()),

time: 169 us -> 166 us (0.982)
  other arithmetic: 3.99 us -> 0 us
where the time goes in v3:
time: 166 us
  Pallas kernels  158 us (95%)
  local copies, waits for them, and re-layouts  6.78 us (4%)
    pallas_call x1, Pallas kernels, halo_body(): pl.pallas_call(functools.partial(wave_kernel, (own, nspec, nrow, ncol, mo...  158 us
    unnamed x1, local copies, waits for them, and re-layouts  6.78 us

profile of v3, /device:TPU:0, one launch (start us, length us, event | category | flops | bytes accessed | tf_op | source)
XLA Modules:
  0.0 165.7 jit_solution(6233912553152553338)
XLA Ops:
  0.7 158.3 %shard_map.100 = f32[9,48,16,256]{3,2,1,0:T(8,128)} custom-call(f32[9,48,16,256]{3,2,1,0:T(8,128)} %bitcast.3, f32[1,1,1,1024]{3,2,1,0:T(1,128)} %speed_in.1, f32[1,1,1,1024]{3,2,1,0:T(1,128)} %dir_in.1, s32[1,1,1,1024]{3,2,1,0:T(1,128)} %ice_in.1, s32[1,1,1,1024]{3,2,1,0:T(1,128)} %depth_in.1, s32[1,1,1,768]{3,2,1,0:T(1,128)} %slots_in.1, ...), custom_call_target="tpu_custom_call" | custom-call | tf_op jit(solution)/shard_map/pallas_call | solution.py:577
  158.9 6.8 %copy.13 = f32[432,16,256]{2,1,0:T(8,128)} copy(f32[432,16,256]{2,1,0:T(8,128)} %bitcast.2) | data formatting | bytes 14155776
